TPU v7x, 32 devices: a whole 2x2x4 slice. The times are simulated.
32 devices in a mesh: member: 8 (over z, core), state: 4 (over y, x).
Axes of the slice: x: 2, y: 2, z: 4, core: 2. Of those that a mesh axis runs over, the one named last changes fastest.
Arguments:
- prior_analyses: float32 [64, 256, 1024], P('member', 'state'), may hold values from -6 to 6
- smoothing_number: float32 [256, 1024], P('state'), may hold values from 0.08 to 0.24
- observations: float32 [3072], replicated, may hold values from -6 to 6
- obs_variance: float32 [3072], replicated, may hold values from 0.25 to 2
- obs_row: int32 [3072], replicated, may hold values from 0 to 255
- obs_col: int32 [3072], replicated, may hold values from 0 to 1023
- obs_radius: int32 [3072], replicated, may hold values from 32 to 127
- block_order: int32 [3072], replicated, may hold values from 0 to 3071, each once
Outputs:
- analysis: float32 [64, 256, 1024], P('member', 'state')
Inputs may be any that keep to these rules, and one draw needn't show every extreme that they name: `block_order`: every observation index appears exactly once.
All inputs are finite; a program needn't handle non-finite values.
Results may differ from a plain program's by a relative error of at most 0.0035.
Values sent between devices are 32-bit elements; how exact they have to be, the bound alone decides.
A program may use at most 64 MiB of HBM per device.

v0:
```python
import jax
import jax.numpy as jnp
from jax import lax
from jax.sharding import PartitionSpec as P

BLK = 512
NBLK = 6
spread_eps = 1e-06


def extended(shard, sides, width):
    for axis, dim in sides:
        peers, length = (lax.axis_size(axis), shard.shape[dim])
        up = [(i, (i + 1) % peers) for i in range(peers - 1)]
        down = [(j, i) for i, j in up]
        last = lax.slice_in_dim(shard, length - width, length, axis=dim)
        leading = lax.slice_in_dim(shard, 0, width, axis=dim)
        before = lax.ppermute(last, axis, up)
        after = lax.ppermute(leading, axis, down)
        shard = jnp.concatenate([before, shard, after], axis=dim)
    return shard


def advance(padded, spreading_coefficients):
    center = padded[:, 1:-1, :]
    vertical = padded[:, 2:, :] + padded[:, :-2, :]
    sideways = jnp.pad(center[:, :, 1:], ((0, 0), (0, 0), (0, 1))) + jnp.pad(
        center[:, :, :-1], ((0, 0), (0, 0), (1, 0))
    )
    return center + spreading_coefficients * (vertical + sideways - 4.0 * center)


def predicted_level(realization_vectors, spreading_coefficients):
    current = realization_vectors
    for step_index in range(2):
        padded = extended(current, (("state", 1),), 1)
        current = advance(padded, spreading_coefficients)
    return current


def increments(prior_values, value_array, variances):
    realization_vectors = prior_values.shape[0]
    prior_mean = jnp.mean(prior_values, axis=0)
    anomaly = prior_values - prior_mean
    spread = jnp.sum(anomaly * anomaly, axis=0) / (realization_vectors - 1) + spread_eps
    post_var = spread * variances / (spread + variances)
    posterior_average = post_var * (prior_mean / spread + value_array / variances)
    shrink = jnp.sqrt(variances / (variances + spread)) - 1.0
    increment = (posterior_average - prior_mean + shrink * anomaly).astype(jnp.bfloat16)
    return (anomaly.astype(jnp.bfloat16), increment, 1.0 / spread)


def taper_weight(cell_row, cell_col, obs_rows, obs_cols, radius):
    row_gap = cell_row[None, :] - obs_rows[:, None]
    col_gap = cell_col[None, :] - obs_cols[:, None]
    distance = (row_gap * row_gap + col_gap * col_gap).astype(jnp.float32)
    reach = radius.astype(jnp.float32)
    closeness = jnp.maximum(1.0 - distance / (reach * reach)[:, None], 0.0)
    return closeness * closeness


def linear_gain_fit(
    target, target_rows, target_cols, anomaly, increment, inverse, obs_rows, obs_cols, radius
):
    realization_vectors = target.shape[0]
    cell_mean = jnp.mean(target, axis=0)
    cell_anomaly = (target - cell_mean).astype(jnp.bfloat16)
    sub_size = min(anomaly.shape[1], 128)
    accumulated = jnp.zeros(target.shape, jnp.float32)
    for part_index in range(anomaly.shape[1] // sub_size):
        lower_end = part_index * sub_size
        upper_end = lower_end + sub_size
        covariance = lax.dot_general(
            anomaly[:, lower_end:upper_end],
            cell_anomaly,
            (((0,), (0,)), ((), ())),
            preferred_element_type=jnp.float32,
        ) / (realization_vectors - 1)
        weight = taper_weight(
            target_rows,
            target_cols,
            obs_rows[lower_end:upper_end],
            obs_cols[lower_end:upper_end],
            radius[lower_end:upper_end],
        )
        gain_tile = (weight * covariance * inverse[lower_end:upper_end, None]).astype(jnp.bfloat16)
        accumulated = accumulated + jnp.dot(
            increment[:, lower_end:upper_end], gain_tile, preferred_element_type=jnp.float32
        )
    return accumulated


def pick_values(cell_values, rows_wanted, cols_wanted, first_row, tile_rows, tile_cols):
    local_row = rows_wanted - first_row
    inside = (
        (local_row >= 0) & (local_row < tile_rows) & (cols_wanted >= 0) & (cols_wanted < tile_cols)
    )
    local_index = jnp.where(inside, local_row * tile_cols + cols_wanted, 0)
    return jnp.where(inside[None, :], jnp.take(cell_values, local_index, axis=1), 0.0)


def on_device(
    prior_analyses,
    smoothing_number,
    observations,
    obs_variance,
    obs_row,
    obs_col,
    obs_radius,
    block_order,
):
    realization_vectors = predicted_level(prior_analyses, smoothing_number)
    row_count = realization_vectors.shape[1]
    col_count = realization_vectors.shape[2]
    member_count = lax.axis_size("member")
    base_row = lax.axis_index("state") * row_count
    tile_data = lax.all_to_all(
        realization_vectors, "member", split_axis=1, concat_axis=0, tiled=True
    )
    tile_rows = row_count // member_count
    first_row = base_row + lax.axis_index("member") * tile_rows
    grid_point_total = tile_rows * col_count
    cell_values = tile_data.reshape(tile_data.shape[0], grid_point_total)
    position = jnp.arange(grid_point_total, dtype=jnp.int32)
    cell_row = first_row + position // col_count
    cell_col = position % col_count
    for block_index in range(NBLK):
        chosen = block_order[block_index * BLK : (block_index + 1) * BLK]
        block_rows = jnp.take(obs_row, chosen)
        block_cols = jnp.take(obs_col, chosen)
        block_radius = jnp.take(obs_radius, chosen)
        local_values = pick_values(
            cell_values, block_rows, block_cols, first_row, tile_rows, col_count
        )
        prior_values = lax.psum(local_values, ("member", "state"))
        anomaly, increment, inverse = increments(
            prior_values, jnp.take(observations, chosen), jnp.take(obs_variance, chosen)
        )
        cell_values = cell_values + linear_gain_fit(
            cell_values,
            cell_row,
            cell_col,
            anomaly,
            increment,
            inverse,
            block_rows,
            block_cols,
            block_radius,
        )
    result = cell_values.reshape(tile_data.shape)
    return lax.all_to_all(result, "member", split_axis=0, concat_axis=1, tiled=True)


def solution(mesh):
    in_specs = (P("member", "state", None), P("state", None), P(), P(), P(), P(), P(), P())
    out_specs = P("member", "state", None)
    return jax.shard_map(
        on_device, mesh=mesh, in_specs=in_specs, out_specs=out_specs, check_vma=False
    )
```

profile of v0, /device:TPU:0, one launch (start us, length us, event | category | flops | bytes accessed | tf_op | source)
XLA Modules:
  0.0 1187.5 jit_solution(11396176168441743626)
XLA Ops:
  9.4 4.8 collective-permute-start.1
  107.2 4.3 gather_fusion.34
  111.4 4.2 gather_fusion.33
  119.0 4.5 collective-permute-start.3
  132.1 4.9 all-to-all-start
  140.1 45.9 %all-to-all-done = f32[8,64,1024]{2,0,1:T(8,128)S(1)} async-done(((f32[8,64,1024]{2,0,1:T(8,128)}), f32[8,64,1024]{2,0,1:T(8,128)S(1)}, u32[]{:S(2)}, u32[]{:S(2)}) %all-to-all-start) | async-done | bytes 2097184 | tf_op jit(solution)/shard_map/all_to_all | solution.py:117
  193.2 124.2 %all-reduce.11.cloned.1.call-done = f32[64,512]{0,1:T(8,128)} async-done(((f32[64,512]{0,1:T(8,128)}), f32[64,512]{0,1:T(8,128)}) %all-reduce.11.cloned.1.call-update) | async-done | bytes 131088 | tf_op jit(solution)/shard_map/psum | solution.py:135
  324.9 5.6 convolution_add_fusion.17
  330.4 5.6 convolution_add_fusion.16
  336.0 5.7 fusion.292
  341.7 4.0 copy.34
  350.1 123.9 %all-reduce.13.cloned.1.call-done = f32[64,512]{0,1:T(8,128)} async-done(((f32[64,512]{0,1:T(8,128)}), f32[64,512]{0,1:T(8,128)}) %all-reduce.13.cloned.1.call-update) | async-done | bytes 131088 | tf_op jit(solution)/shard_map/psum | solution.py:135
  481.4 5.6 convolution_add_fusion.14
  487.0 5.6 convolution_add_fusion.13
  492.6 5.7 fusion.295
  506.7 123.9 %all-reduce.15.cloned.1.call-done = f32[64,512]{0,1:T(8,128)} async-done(((f32[64,512]{0,1:T(8,128)}), f32[64,512]{0,1:T(8,128)}) %all-reduce.15.cloned.1.call-update) | async-done | bytes 131088 | tf_op jit(solution)/shard_map/psum | solution.py:135
  638.0 5.6 convolution_add_fusion.11
  643.6 5.6 convolution_add_fusion.10
  649.2 5.6 fusion.298
  662.2 123.7 %all-reduce.17.cloned.1.call-done = f32[64,512]{0,1:T(8,128)} async-done(((f32[64,512]{0,1:T(8,128)}), f32[64,512]{0,1:T(8,128)}) %all-reduce.17.cloned.1.call-update) | async-done | bytes 131088 | tf_op jit(solution)/shard_map/psum | solution.py:135
  793.3 5.6 convolution_add_fusion.8
  798.9 5.6 convolution_add_fusion.7
  804.4 5.7 fusion.301
  818.5 123.9 %all-reduce.19.cloned.1.call-done = f32[64,512]{0,1:T(8,128)} async-done(((f32[64,512]{0,1:T(8,128)}), f32[64,512]{0,1:T(8,128)}) %all-reduce.19.cloned.1.call-update) | async-done | bytes 131088 | tf_op jit(solution)/shard_map/psum | solution.py:135
  949.9 5.6 convolution_add_fusion.5
  955.5 5.6 convolution_add_fusion.4
  961.0 5.7 fusion.304
  975.2 124.1 %all-reduce.21.cloned.1.call-done = f32[64,512]{0,1:T(8,128)} async-done(((f32[64,512]{0,1:T(8,128)}), f32[64,512]{0,1:T(8,128)}) %all-reduce.21.cloned.1.call-update) | async-done | bytes 131088 | tf_op jit(solution)/shard_map/psum | solution.py:135
  1106.9 5.6 convolution_add_fusion.2
  1112.5 5.6 convolution_add_fusion.1
  1118.1 5.7 fusion.72
  1126.6 52.4 %all_to_all.33 = f32[64,8,1024]{2,1,0:T(8,128)S(1)} all-to-all(f32[64,8,1024]{2,1,0:T(8,128)S(1)} %bitcast.36), channel_id=1, replica_groups=mesh['member'=8,'state'=4] {'member'}, dimensions={0} | all-to-all | bytes 4194304 | tf_op jit(solution)/shard_map/all_to_all | solution.py:151
  (221 shorter events, 202.9 us)
Async XLA Ops:
  6.5 11.9 copy-start
  9.4 106.3 %collective-permute-start.1 = (f32[8,1,1024]{2,0,1:T(8,128)S(1)}, f32[8,1,1024]{2,0,1:T(8,128)S(1)}, u32[]{:S(2)}, u32[]{:S(2)}) collective-permute-start(f32[8,1,1024]{2,0,1:T(8,128)S(1)} %get-tuple-element.57), channel_id=1, source_target_pairs={{0,1},{1,2},{2,3},{4,5},{5,6},{6,7},{8,9},{9,10},{10,11},{12,13},{... | collective-permute-start | bytes 98312 | tf_op jit(solution)/shard_map/ppermute | solution.py:18
  14.2 101.4 %collective-permute-start = (f32[8,1,1024]{2,0,1:T(8,128)S(1)}, f32[8,1,1024]{2,0,1:T(8,128)S(1)}, u32[]{:S(2)}, u32[]{:S(2)}) collective-permute-start(f32[8,1,1024]{2,0,1:T(8,128)S(1)} %get-tuple-element.56), channel_id=1, source_target_pairs={{1,0},{2,1},{3,2},{5,4},{6,5},{7,6},{9,8},{10,9},{11,10},{13,12},{... | collective-permute-start | bytes 98312 | tf_op jit(solution)/shard_map/ppermute | solution.py:19
  18.3 6.5 copy-start.2
  18.4 12.8 %copy-start.3 = (s32[3072]{0:T(1024)S(1)}, s32[3072]{0:T(1024)}, u32[]{:S(2)}) copy-start(s32[3072]{0:T(1024)} %param.19) | copy-start | bytes 36868
  50.1 12.9 %copy-start.4 = (f32[3072]{0:T(1024)S(1)}, f32[3072]{0:T(1024)}, u32[]{:S(2)}) copy-start(f32[3072]{0:T(1024)} %param.16) | copy-start | bytes 36868
  56.5 12.9 %copy-start.5 = (f32[3072]{0:T(1024)S(1)}, f32[3072]{0:T(1024)}, u32[]{:S(2)}) copy-start(f32[3072]{0:T(1024)} %param.17) | copy-start | bytes 36868
  62.8 74.2 %copy-start.15 = (pred[512]{0:T(512)(128)(4,1)}, pred[512]{0:T(512)(128)(4,1)S(1)}, u32[]{:S(2)}) copy-start(pred[512]{0:T(512)(128)(4,1)S(1)} %get-tuple-element.8) | copy-start | bytes 1540
  100.8 14.8 %copy-start.10 = (f32[64,1024]{1,0:T(8,128)S(1)}, f32[64,1024]{1,0:T(8,128)}, u32[]{:S(2)}) copy-start(f32[64,1024]{1,0:T(8,128)} %param.15) | copy-start | bytes 786436
  119.0 7.1 collective-permute-start.3
  123.6 6.2 collective-permute-start.2
  132.1 53.9 %all-to-all-start = ((f32[8,64,1024]{2,0,1:T(8,128)}), f32[8,64,1024]{2,0,1:T(8,128)S(1)}, u32[]{:S(2)}, u32[]{:S(2)}) async-start(f32[8,64,1024]{2,0,1:T(8,128)} %fusion.82), calls=%async_computation | async-start | bytes 4194304 | tf_op jit(solution)/shard_map/all_to_all | solution.py:117
  137.0 180.5 %all-reduce.11.cloned.1.call-start = ((), (), s32[]{:S(2)}) async-start(), calls=%async_computation.2 | async-start | bytes 524288 | tf_op jit(solution)/shard_map/psum | solution.py:135
  192.9 281.1 %all-reduce.13.cloned.1.call-start = ((), (), s32[]{:S(2)}) async-start(), calls=%async_computation.3 | async-start | bytes 524288 | tf_op jit(solution)/shard_map/psum | solution.py:135
  341.7 135.8 %copy-start.6 = (f32[64,8192]{1,0:T(8,128)S(1)}, f32[64,8192]{1,0:T(8,128)}, u32[]{:S(2)}) copy-start(f32[64,8192]{1,0:T(8,128)} %get-tuple-element.201) | copy-start | bytes 6291460
  349.8 280.7 %all-reduce.15.cloned.1.call-start = ((), (), s32[]{:S(2)}) async-start(), calls=%async_computation.4 | async-start | bytes 524288 | tf_op jit(solution)/shard_map/psum | solution.py:135
  498.3 135.8 %copy-start.7 = (f32[64,8192]{1,0:T(8,128)S(1)}, f32[64,8192]{1,0:T(8,128)}, u32[]{:S(2)}) copy-start(f32[64,8192]{1,0:T(8,128)} %get-tuple-element.203) | copy-start | bytes 6291460
  506.4 279.5 %all-reduce.17.cloned.1.call-start = ((), (), s32[]{:S(2)}) async-start(), calls=%async_computation.5 | async-start | bytes 524288 | tf_op jit(solution)/shard_map/psum | solution.py:135
  661.7 280.7 %all-reduce.19.cloned.1.call-start = ((), (), s32[]{:S(2)}) async-start(), calls=%async_computation.6 | async-start | bytes 524288 | tf_op jit(solution)/shard_map/psum | solution.py:135
  810.2 135.8 %copy-start.8 = (f32[64,8192]{1,0:T(8,128)S(1)}, f32[64,8192]{1,0:T(8,128)}, u32[]{:S(2)}) copy-start(f32[64,8192]{1,0:T(8,128)} %get-tuple-element.207) | copy-start | bytes 6291460
  818.3 281.0 %all-reduce.21.cloned.1.call-start = ((), (), s32[]{:S(2)}) async-start(), calls=%async_computation.7 | async-start | bytes 524288 | tf_op jit(solution)/shard_map/psum | solution.py:135
  966.8 7.5 copy-start.17
  966.8 7.5 copy-start.18
  966.8 134.8 %copy-start.13 = (f32[512]{0:T(512)S(1)}, f32[512]{0:T(512)}, u32[]{:S(2)}) copy-start(f32[512]{0:T(512)} %gather_fusion.34) | copy-start | bytes 6148
  966.8 134.8 %copy-start.14 = (f32[512]{0:T(512)S(1)}, f32[512]{0:T(512)}, u32[]{:S(2)}) copy-start(f32[512]{0:T(512)} %gather_fusion.33) | copy-start | bytes 6148
  966.8 134.8 %copy-start.16 = (pred[512]{0:T(512)(128)(4,1)S(1)}, pred[512]{0:T(512)(128)(4,1)}, u32[]{:S(2)}) copy-start(pred[512]{0:T(512)(128)(4,1)} %copy-done.15) | copy-start | bytes 1540
  966.8 136.1 %copy-start.9 = (f32[64,8192]{1,0:T(8,128)S(1)}, f32[64,8192]{1,0:T(8,128)}, u32[]{:S(2)}) copy-start(f32[64,8192]{1,0:T(8,128)} %get-tuple-element.209) | copy-start | bytes 6291460
  966.8 136.1 %copy-start.25 = (s32[128]{0:T(128)S(1)}, s32[128]{0:T(128)}, u32[]{:S(2)}) copy-start(s32[128]{0:T(128)} %get-tuple-element.101) | copy-start | bytes 1540
  966.8 136.1 %copy-start.26 = (s32[128]{0:T(128)S(1)}, s32[128]{0:T(128)}, u32[]{:S(2)}) copy-start(s32[128]{0:T(128)} %get-tuple-element.237) | copy-start | bytes 1540
  966.8 136.1 %copy-start.30 = (f32[128]{0:T(128)S(1)}, f32[128]{0:T(128)}, u32[]{:S(2)}) copy-start(f32[128]{0:T(128)} %get-tuple-element.109) | copy-start | bytes 1540
  1112.5 5.6 copy-start.19
  1126.6 53.9 %copy-start.1 = (s32[3072]{0:T(1024)S(1)}, s32[3072]{0:T(1024)}, u32[]{:S(2)}) copy-start(s32[3072]{0:T(1024)} %param.20) | copy-start | bytes 36868
  (10 other events, 47.9 us)
Sparse Core Ops, SparseCore 0:
  193.0 124.3 all-reduce.10
  350.0 123.9 all-reduce.12
  506.5 123.9 all-reduce.14
  661.9 123.9 all-reduce.16
  818.4 123.9 all-reduce.18
  975.3 123.9 all-reduce.20
where the time goes:
time: 1190 us
  waiting for transfers between devices  793 us (67%)
  local copies, waits for them, and re-layouts  149 us (13%)
  matrix products  125 us (11%)
  blocking collectives  52.4 us (4%)
  other arithmetic  34.9 us (3%)
  starting transfers between devices  18.5 us (2%)
  between operations  14.9 us (1%)
    psum x6, waiting for transfers between devices, on_device(): prior_values = lax.psum(local_values, ('member', 'state'))  744 us
    dot_general x24, matrix products, linear_gain_fit(): jnp.dot(increment[:, lower_end:upper_end], gain_tile, preferred_element_t...  125 us
    all_to_all x1, blocking collectives, on_device(): lax.all_to_all(result, 'member', split_axis=0, concat_axis=1, tiled=True)  52.4 us
    all_to_all x1, waiting for transfers between devices, on_device(): lax.all_to_all(realization_vectors, 'member', split_axis=1, concat_axis=0...  45.9 us
  transfers between devices with their start and end apart: 11, of which 8 were waited for; matrix products, arithmetic and copies ran while one was open for 9% of the time, Pallas kernels for 0%

commit v1 on v0

--- a/solution.py
+++ b/solution.py
@@ -132,7 +132,7 @@
         local_values = pick_values(
             cell_values, block_rows, block_cols, first_row, tile_rows, col_count
         )
-        prior_values = lax.psum(local_values, ("member", "state"))
+        prior_values = lax.psum(lax.psum(local_values, "state"), "member")
         anomaly, increment, inverse = increments(
             prior_values, jnp.take(observations, chosen), jnp.take(obs_variance, chosen)
         )

time: 1190 us -> 1010 us (0.85)
  waiting for transfers between devices: 793 us -> 606 us
    psum x6 -> x12, waiting for transfers between devices: 744 us -> 556 us  [on_device(): prior_values = lax.psum(lax.psum(local_values, 'state'), 'member')]
  transfers between devices with their start and end apart: 11 -> 17, of which waited for: 8 -> 14; matrix products, arithmetic and copies ran while one was open for 9% -> 10% of each run, Pallas kernels for 0% -> 0%
where the time goes in v1:
time: 1010 us; the launch traced here: 996 us
  waiting for transfers between devices  606 us (60%)
  local copies, waits for them, and re-layouts  146 us (14%)
  matrix products  124 us (12%)
  blocking collectives  51.5 us (5%)
  other arithmetic  34.4 us (3%)
  starting transfers between devices  18.9 us (2%)
  between operations  15.1 us (1%)
    psum x12, waiting for transfers between devices, on_device(): prior_values = lax.psum(lax.psum(local_values, 'state'), 'member')  556 us
    dot_general x24, matrix products, linear_gain_fit(): jnp.dot(increment[:, lower_end:upper_end], gain_tile, preferred_element_t...  124 us
    all_to_all x1, blocking collectives, on_device(): lax.all_to_all(result, 'member', split_axis=0, concat_axis=1, tiled=True)  51.5 us
    all_to_all x1, waiting for transfers between devices, on_device(): lax.all_to_all(realization_vectors, 'member', split_axis=1, concat_axis=0...  46.1 us
  transfers between devices with their start and end apart: 17, of which 14 were waited for; matrix products, arithmetic and copies ran while one was open for 10% of the time, Pallas kernels for 0%

profile of v1, /device:TPU:0, one launch (start us, length us, event | category | flops | bytes accessed | tf_op | source)
XLA Modules:
  0.0 996.3 jit_solution(7791865165341800871)
XLA Ops:
  100.1 46.1 %all-to-all-done = f32[8,64,1024]{2,0,1:T(8,128)S(1)} async-done(((f32[8,64,1024]{2,0,1:T(8,128)}), f32[8,64,1024]{2,0,1:T(8,128)S(1)}, u32[]{:S(2)}, u32[]{:S(2)}) %all-to-all-start) | async-done | bytes 2097184 | tf_op jit(solution)/shard_map/all_to_all | solution.py:117
  159.7 35.9 %all-reduce.17.cloned.1.call-done = f32[64,512]{0,1:T(8,128)} async-done(((f32[64,512]{0,1:T(8,128)}), f32[64,512]{0,1:T(8,128)}) %all-reduce.17.cloned.1.call-update) | async-done | bytes 131088 | tf_op jit(solution)/shard_map/psum | solution.py:135
  195.7 57.2 %all-reduce.19.cloned.1.call-done = f32[64,512]{0,1:T(8,128)} async-done(((f32[64,512]{0,1:T(8,128)}), f32[64,512]{0,1:T(8,128)}) %all-reduce.19.cloned.1.call-update) | async-done | bytes 131088 | tf_op jit(solution)/shard_map/psum | solution.py:135
  260.4 5.6 convolution_add_fusion.17
  265.9 5.5 convolution_add_fusion.16
  271.5 5.7 fusion.292
  291.7 35.7 %all-reduce.21.cloned.1.call-done = f32[64,512]{0,1:T(8,128)} async-done(((f32[64,512]{0,1:T(8,128)}), f32[64,512]{0,1:T(8,128)}) %all-reduce.21.cloned.1.call-update) | async-done | bytes 131088 | tf_op jit(solution)/shard_map/psum | solution.py:135
  327.6 56.9 %all-reduce.23.cloned.1.call-done = f32[64,512]{0,1:T(8,128)} async-done(((f32[64,512]{0,1:T(8,128)}), f32[64,512]{0,1:T(8,128)}) %all-reduce.23.cloned.1.call-update) | async-done | bytes 131088 | tf_op jit(solution)/shard_map/psum | solution.py:135
  392.0 5.6 convolution_add_fusion.14
  397.6 5.5 convolution_add_fusion.13
  403.1 5.7 fusion.295
  423.4 35.7 %all-reduce.25.cloned.1.call-done = f32[64,512]{0,1:T(8,128)} async-done(((f32[64,512]{0,1:T(8,128)}), f32[64,512]{0,1:T(8,128)}) %all-reduce.25.cloned.1.call-update) | async-done | bytes 131088 | tf_op jit(solution)/shard_map/psum | solution.py:135
  459.3 56.9 %all-reduce.27.cloned.1.call-done = f32[64,512]{0,1:T(8,128)} async-done(((f32[64,512]{0,1:T(8,128)}), f32[64,512]{0,1:T(8,128)}) %all-reduce.27.cloned.1.call-update) | async-done | bytes 131088 | tf_op jit(solution)/shard_map/psum | solution.py:135
  523.7 5.6 convolution_add_fusion.11
  529.3 5.6 convolution_add_fusion.10
  534.9 5.6 fusion.298
  553.8 35.7 %all-reduce.29.cloned.1.call-done = f32[64,512]{0,1:T(8,128)} async-done(((f32[64,512]{0,1:T(8,128)}), f32[64,512]{0,1:T(8,128)}) %all-reduce.29.cloned.1.call-update) | async-done | bytes 131088 | tf_op jit(solution)/shard_map/psum | solution.py:135
  590.0 56.8 %all-reduce.31.cloned.1.call-done = f32[64,512]{0,1:T(8,128)} async-done(((f32[64,512]{0,1:T(8,128)}), f32[64,512]{0,1:T(8,128)}) %all-reduce.31.cloned.1.call-update) | async-done | bytes 131088 | tf_op jit(solution)/shard_map/psum | solution.py:135
  654.3 5.6 convolution_add_fusion.8
  659.9 5.6 convolution_add_fusion.7
  665.5 5.6 fusion.301
  690.9 29.2 %all-reduce.33.cloned.1.call-done = f32[64,512]{0,1:T(8,128)} async-done(((f32[64,512]{0,1:T(8,128)}), f32[64,512]{0,1:T(8,128)}) %all-reduce.33.cloned.1.call-update) | async-done | bytes 131088 | tf_op jit(solution)/shard_map/psum | solution.py:135
  720.2 57.1 %all-reduce.35.cloned.1.call-done = f32[64,512]{0,1:T(8,128)} async-done(((f32[64,512]{0,1:T(8,128)}), f32[64,512]{0,1:T(8,128)}) %all-reduce.35.cloned.1.call-update) | async-done | bytes 131088 | tf_op jit(solution)/shard_map/psum | solution.py:135
  784.7 5.5 convolution_add_fusion.5
  790.3 5.6 convolution_add_fusion.4
  795.8 5.7 fusion.304
  810.0 41.8 %all-reduce.37.cloned.1.call-done = f32[64,512]{0,1:T(8,128)} async-done(((f32[64,512]{0,1:T(8,128)}), f32[64,512]{0,1:T(8,128)}) %all-reduce.37.cloned.1.call-update) | async-done | bytes 131088 | tf_op jit(solution)/shard_map/psum | solution.py:135
  851.8 57.1 %all-reduce.39.cloned.1.call-done = f32[64,512]{0,1:T(8,128)} async-done(((f32[64,512]{0,1:T(8,128)}), f32[64,512]{0,1:T(8,128)}) %all-reduce.39.cloned.1.call-update) | async-done | bytes 131088 | tf_op jit(solution)/shard_map/psum | solution.py:135
  916.5 5.6 convolution_add_fusion.2
  922.1 5.6 convolution_add_fusion.1
  927.6 5.7 fusion.72
  936.1 51.5 %all_to_all.33 = f32[64,8,1024]{2,1,0:T(8,128)S(1)} all-to-all(f32[64,8,1024]{2,1,0:T(8,128)S(1)} %bitcast.36), channel_id=1, replica_groups=mesh['member'=8,'state'=4] {'member'}, dimensions={0} | all-to-all | bytes 4194304 | tf_op jit(solution)/shard_map/all_to_all | solution.py:151
  (231 shorter events, 226.8 us)
Async XLA Ops:
  6.5 11.9 %copy-start = (s32[3072]{0:T(1024)S(1)}, s32[3072]{0:T(1024)}, u32[]{:S(2)}) copy-start(s32[3072]{0:T(1024)} %param.20) | copy-start | bytes 36868
  9.4 66.4 %collective-permute-start.1 = (f32[8,1,1024]{2,0,1:T(8,128)S(1)}, f32[8,1,1024]{2,0,1:T(8,128)S(1)}, u32[]{:S(2)}, u32[]{:S(2)}) collective-permute-start(f32[8,1,1024]{2,0,1:T(8,128)S(1)} %get-tuple-element.57), channel_id=1, source_target_pairs={{0,1},{1,2},{2,3},{4,5},{5,6},{6,7},{8,9},{9,10},{10,11},{12,13},{... | collective-permute-start | bytes 98312 | tf_op jit(solution)/shard_map/ppermute | solution.py:18
  14.2 61.6 %collective-permute-start = (f32[8,1,1024]{2,0,1:T(8,128)S(1)}, f32[8,1,1024]{2,0,1:T(8,128)S(1)}, u32[]{:S(2)}, u32[]{:S(2)}) collective-permute-start(f32[8,1,1024]{2,0,1:T(8,128)S(1)} %get-tuple-element.56), channel_id=1, source_target_pairs={{1,0},{2,1},{3,2},{5,4},{6,5},{7,6},{9,8},{10,9},{11,10},{13,12},{... | collective-permute-start | bytes 98312 | tf_op jit(solution)/shard_map/ppermute | solution.py:19
  24.7 12.7 %copy-start.2 = (s32[3072]{0:T(1024)S(1)}, s32[3072]{0:T(1024)}, u32[]{:S(2)}) copy-start(s32[3072]{0:T(1024)} %param.18) | copy-start | bytes 36868
  27.9 12.7 %copy-start.3 = (s32[3072]{0:T(1024)S(1)}, s32[3072]{0:T(1024)}, u32[]{:S(2)}) copy-start(s32[3072]{0:T(1024)} %param.19) | copy-start | bytes 36868
  44.3 54.1 %copy-start.13 = (pred[512]{0:T(512)(128)(4,1)}, pred[512]{0:T(512)(128)(4,1)S(1)}, u32[]{:S(2)}) copy-start(pred[512]{0:T(512)(128)(4,1)S(1)} %get-tuple-element.8) | copy-start | bytes 1540
  63.2 12.6 %copy-start.10 = (f32[64,1024]{1,0:T(8,128)S(1)}, f32[64,1024]{1,0:T(8,128)}, u32[]{:S(2)}) copy-start(f32[64,1024]{1,0:T(8,128)} %param.15) | copy-start | bytes 786436
  79.2 6.7 collective-permute-start.3
  83.7 6.2 collective-permute-start.2
  92.3 53.9 %all-to-all-start = ((f32[8,64,1024]{2,0,1:T(8,128)}), f32[8,64,1024]{2,0,1:T(8,128)S(1)}, u32[]{:S(2)}, u32[]{:S(2)}) async-start(f32[8,64,1024]{2,0,1:T(8,128)} %fusion.82), calls=%async_computation | async-start | bytes 4194304 | tf_op jit(solution)/shard_map/all_to_all | solution.py:117
  97.2 98.4 %all-reduce.17.cloned.1.call-start = ((), (), s32[]{:S(2)}) async-start(), calls=%async_computation.2 | async-start | bytes 524288 | tf_op jit(solution)/shard_map/psum | solution.py:135
  97.7 55.5 %copy-start.4 = (f32[3072]{0:T(1024)S(1)}, f32[3072]{0:T(1024)}, u32[]{:S(2)}) copy-start(f32[3072]{0:T(1024)} %param.16) | copy-start | bytes 36868
  146.2 10.1 %copy-start.5 = (f32[3072]{0:T(1024)S(1)}, f32[3072]{0:T(1024)}, u32[]{:S(2)}) copy-start(f32[3072]{0:T(1024)} %param.17) | copy-start | bytes 36868
  153.1 99.8 %all-reduce.19.cloned.1.call-start = ((), (), s32[]{:S(2)}) async-start(), calls=%async_computation.3 | async-start | bytes 524288 | tf_op jit(solution)/shard_map/psum | solution.py:135
  195.6 131.8 %all-reduce.21.cloned.1.call-start = ((), (), s32[]{:S(2)}) async-start(), calls=%async_computation.4 | async-start | bytes 524288 | tf_op jit(solution)/shard_map/psum | solution.py:135
  281.0 107.1 %copy-start.6 = (f32[64,8192]{1,0:T(8,128)S(1)}, f32[64,8192]{1,0:T(8,128)}, u32[]{:S(2)}) copy-start(f32[64,8192]{1,0:T(8,128)} %get-tuple-element.201) | copy-start | bytes 6291460
  285.3 99.3 %all-reduce.23.cloned.1.call-start = ((), (), s32[]{:S(2)}) async-start(), calls=%async_computation.5 | async-start | bytes 524288 | tf_op jit(solution)/shard_map/psum | solution.py:135
  327.4 131.6 %all-reduce.25.cloned.1.call-start = ((), (), s32[]{:S(2)}) async-start(), calls=%async_computation.6 | async-start | bytes 524288 | tf_op jit(solution)/shard_map/psum | solution.py:135
  412.7 107.1 %copy-start.8 = (f32[64,8192]{1,0:T(8,128)S(1)}, f32[64,8192]{1,0:T(8,128)}, u32[]{:S(2)}) copy-start(f32[64,8192]{1,0:T(8,128)} %get-tuple-element.203) | copy-start | bytes 6291460
  417.0 99.2 %all-reduce.27.cloned.1.call-start = ((), (), s32[]{:S(2)}) async-start(), calls=%async_computation.7 | async-start | bytes 524288 | tf_op jit(solution)/shard_map/psum | solution.py:135
  459.1 130.5 %all-reduce.29.cloned.1.call-start = ((), (), s32[]{:S(2)}) async-start(), calls=%async_computation.8 | async-start | bytes 524288 | tf_op jit(solution)/shard_map/psum | solution.py:135
  540.5 119.4 %copy-start.7 = (f32[64,8192]{1,0:T(8,128)}, f32[64,8192]{1,0:T(8,128)S(1)}, u32[]{:S(2)}) copy-start(f32[64,8192]{1,0:T(8,128)S(1)} %get-tuple-element.205) | copy-start | bytes 6291460
  547.4 99.4 %all-reduce.31.cloned.1.call-start = ((), (), s32[]{:S(2)}) async-start(), calls=%async_computation.9 | async-start | bytes 524288 | tf_op jit(solution)/shard_map/psum | solution.py:135
  589.5 130.5 %all-reduce.33.cloned.1.call-start = ((), (), s32[]{:S(2)}) async-start(), calls=%async_computation.10 | async-start | bytes 524288 | tf_op jit(solution)/shard_map/psum | solution.py:135
  678.0 99.2 %all-reduce.35.cloned.1.call-start = ((), (), s32[]{:S(2)}) async-start(), calls=%async_computation.11 | async-start | bytes 524288 | tf_op jit(solution)/shard_map/psum | solution.py:135
  720.1 131.7 %all-reduce.37.cloned.1.call-start = ((), (), s32[]{:S(2)}) async-start(), calls=%async_computation.12 | async-start | bytes 524288 | tf_op jit(solution)/shard_map/psum | solution.py:135
  801.5 109.7 %copy-start.14 = (pred[512]{0:T(512)(128)(4,1)S(1)}, pred[512]{0:T(512)(128)(4,1)}, u32[]{:S(2)}) copy-start(pred[512]{0:T(512)(128)(4,1)} %copy-done.13) | copy-start | bytes 1540
  801.5 111.0 %copy-start.9 = (f32[64,8192]{1,0:T(8,128)S(1)}, f32[64,8192]{1,0:T(8,128)}, u32[]{:S(2)}) copy-start(f32[64,8192]{1,0:T(8,128)} %get-tuple-element.209) | copy-start | bytes 6291460
  801.6 111.0 %copy-start.23 = (s32[128]{0:T(128)S(1)}, s32[128]{0:T(128)}, u32[]{:S(2)}) copy-start(s32[128]{0:T(128)} %get-tuple-element.101) | copy-start | bytes 1540
  801.6 111.0 %copy-start.24 = (s32[128]{0:T(128)S(1)}, s32[128]{0:T(128)}, u32[]{:S(2)}) copy-start(s32[128]{0:T(128)} %get-tuple-element.237) | copy-start | bytes 1540
  809.7 99.3 %all-reduce.39.cloned.1.call-start = ((), (), s32[]{:S(2)}) async-start(), calls=%async_computation.13 | async-start | bytes 524288 | tf_op jit(solution)/shard_map/psum | solution.py:135
  936.1 53.0 %copy-start.1 = (s32[3072]{0:T(1024)S(1)}, s32[3072]{0:T(1024)}, u32[]{:S(2)}) copy-start(s32[3072]{0:T(1024)} %param.20) | copy-start | bytes 36868
  (12 other events, 68.2 us)
Sparse Core Ops, SparseCore 0:
  153.2 42.3 all-reduce.16
  198.0 54.8 all-reduce.18
  285.4 41.9 all-reduce.20
  329.7 54.8 all-reduce.22
  417.1 41.8 all-reduce.24
  461.3 54.8 all-reduce.26
  547.6 41.9 all-reduce.28
  591.9 54.8 all-reduce.30
  678.1 41.9 all-reduce.32
  722.4 54.8 all-reduce.34
  809.8 41.9 all-reduce.36
  854.1 54.8 all-reduce.38
